TPU v7x, 256 devices: a whole 4x4x8 slice. The times are simulated.
256 devices in a mesh: expert: 32 (over y, x, core), tensor: 8 (over z).
Axes of the slice: x: 4, y: 4, z: 8, core: 2. Of those that a mesh axis runs over, the one named last changes fastest.
Arguments:
- tokens: bfloat16 [16384, 4096], P('expert', 'tensor'), may hold values from -36 to 36
- expert_ids: int32 [16384, 1], P('expert'), may hold values from 0 to 63; in each aligned block of 512 rows (0 to 511, 512 to 1023, ...) at most 16 rows name the same one
- gates: float32 [16384, 1], P('expert'), may hold values from 0.25 to 1
- expert_in: bfloat16 [64, 4096, 2048], P('expert', 'tensor'), may hold values from -0.09375 to 0.09375
- expert_out: bfloat16 [64, 2048, 4096], P('expert', None, 'tensor'), may hold values from -0.125 to 0.125
- norm_gain: float32 [4096], replicated, may hold values from 0.5 to 2
- up_weight: bfloat16 [4096, 8192], P('expert', 'tensor'), may hold values from -0.09375 to 0.09375
- down_weight: bfloat16 [4096, 8192], P('expert', 'tensor'), may hold values from -0.0625 to 0.0625
Outputs:
- layer_output: bfloat16 [16384, 4096], P('expert', 'tensor')
Inputs may be any that keep to these rules, and one draw needn't show every extreme that they name: `expert_ids`: among the 512 tokens of one block, at most 16 carry the same expert id; in some blocks one id is carried by exactly 16 tokens.
All inputs are finite; a program needn't handle non-finite values.
Results may differ from a plain program's by a relative error of at most 0.015.
Values may be sent and summed in bfloat16 or wider, within the bound.
No kernel may reach another device: no remote copies, remote signals or barrier semaphores. Data moves between devices by JAX's collectives and lax.ppermute only.
A program may use at most 128 MiB of HBM per device.

v0:
```python
import jax
import jax.numpy as jnp
from jax import lax
from jax.sharding import PartitionSpec as P

EXP_DEV = 2


def slot_table(expert_col, experts, capacity):
    expert = expert_col[:, 0]
    onehot = (expert[:, None] == jnp.arange(experts, dtype=jnp.int32)[None, :]).astype(jnp.int32)
    before = jnp.cumsum(onehot, axis=0) - onehot
    position = jnp.sum(before * onehot, axis=1)
    slot_index = expert * capacity + position
    selector = jnp.arange(experts * capacity, dtype=jnp.int32)[:, None] == slot_index[None, :]
    return selector.astype(jnp.bfloat16)


def trade(buffer):
    result = lax.all_to_all(buffer, "expert", split_axis=0, concat_axis=0, tiled=True)
    return result


def gather_rows(weight, combine, start_value):
    return combine(start_value, lax.all_gather(weight, "expert", axis=0, tiled=True), jnp.int32(0))


def shards(tokens, expert_ids, gates, expert_in, expert_out, norm_gain, up_weight, down_weight):
    token_count = tokens.shape[0]
    local_width = tokens.shape[1]
    groups = lax.axis_size("expert")
    experts = EXP_DEV * groups
    capacity = 2 * token_count // experts
    selector = slot_table(expert_ids, experts, capacity)
    outgoing = jnp.dot(selector, tokens, preferred_element_type=jnp.float32).astype(jnp.bfloat16)
    outgoing = outgoing.reshape(groups, EXP_DEV, capacity, local_width)
    arrived = trade(outgoing)
    partial_value = jnp.einsum(
        "sjcd,jdh->sjch", arrived, expert_in, preferred_element_type=jnp.float32
    )
    summed = lax.psum(partial_value.astype(jnp.bfloat16), "tensor").astype(jnp.float32)
    active = jax.nn.relu(summed).astype(jnp.bfloat16)
    produced = jnp.einsum(
        "sjch,jhd->sjcd", active, expert_out, preferred_element_type=jnp.float32
    ).astype(jnp.bfloat16)
    returned = trade(produced).reshape(experts * capacity, local_width)
    routed = lax.dot_general(
        selector, returned, (((0,), (0,)), ((), ())), preferred_element_type=jnp.float32
    )
    mixed = (tokens.astype(jnp.float32) + gates * routed).astype(jnp.bfloat16)
    whole = lax.all_gather(mixed, "tensor", axis=1, tiled=True)
    whole_f32 = whole.astype(jnp.float32)
    mean_square = jnp.mean(whole_f32 * whole_f32, axis=1, keepdims=True)
    normed = (whole_f32 * lax.rsqrt(mean_square + 1e-06) * norm_gain).astype(jnp.bfloat16)

    def add_up(carry, piece, start):
        return jnp.dot(normed, piece, preferred_element_type=jnp.float32)

    ffn_hidden = gather_rows(
        up_weight, add_up, jnp.zeros((token_count, up_weight.shape[1]), jnp.float32)
    )
    ffn_active = jax.nn.gelu(ffn_hidden, approximate=True).astype(jnp.bfloat16)

    def add_down(carry, piece, start):
        contribution = lax.dot_general(
            ffn_active, piece, (((1,), (1,)), ((), ())), preferred_element_type=jnp.float32
        )
        return contribution

    outputs = gather_rows(
        down_weight, add_down, jnp.zeros((token_count, whole.shape[1]), jnp.float32)
    )
    summed_out = lax.psum_scatter(
        outputs.astype(jnp.bfloat16), "tensor", scatter_dimension=1, tiled=True
    ).astype(jnp.float32)
    return (mixed.astype(jnp.float32) + summed_out).astype(jnp.bfloat16)


def solution(mesh):
    return jax.shard_map(
        shards,
        mesh=mesh,
        in_specs=(
            P("expert", "tensor"),
            P("expert", None),
            P("expert", None),
            P("expert", "tensor", None),
            P("expert", None, "tensor"),
            P(),
            P("expert", "tensor"),
            P("expert", "tensor"),
        ),
        out_specs=P("expert", "tensor"),
        check_vma=False,
    )
```

profile of v0, /device:TPU:1, one launch (start us, length us, event | category | flops | bytes accessed | tf_op | source)
XLA Modules:
  0.0 424.8 jit_solution(10991581283528540992)
XLA Ops:
  6.5 0.0 all-reduce.2.cloned.1.call-start
  6.5 0.7 fusion.42
  7.2 1.2 reduce-window.6
  8.4 0.2 slice_reduce_fusion
  8.7 0.0 copy-start.1
  8.7 0.9 fusion.41
  9.7 0.9 multiply_add_fusion
  10.6 1.8 fusion.24
  12.4 25.6 %all_to_all.10 = bf16[32,2,16,512]{3,2,1,0:T(8,128)(2,1)S(1)} all-to-all(bf16[32,2,16,512]{3,2,1,0:T(8,128)(2,1)S(1)} %bitcast.50), channel_id=1, replica_groups=mesh['expert'=32,'tensor'=8] {'expert'}, dimensions={0} | all-to-all | bytes 2097152 | tf_op jit(solution)/shard_map/all_to_all | solution.py:20
  37.9 0.0 copy-done.1
  37.9 4.3 %convert_bitcast_fusion = bf16[32,2,16,2048]{3,2,0,1:T(8,128)(2,1)} fusion(bf16[2,512,2048]{2,1,0:T(8,128)(2,1)S(1)} %copy-done.1, bf16[32,2,16,512]{3,2,1,0:T(8,128)(2,1)S(1)} %all_to_all.10), kind=kOutput, calls=%fused_computation.15 | convolution fusion | flops 2149580800 | bytes 9437184 | tf_op jit(solution)/shard_map/sjcd,jdh->sjch/dot_general | solution.py:38
  42.2 0.0 all-reduce.2.cloned.1.call-update
  42.3 0.0 all-gather.4.cloned.1.call-start
  42.3 108.1 %all-reduce.2.cloned.1.call-done = bf16[32,2,16,2048]{3,2,0,1:T(8,128)(2,1)} async-done(((bf16[32,2,16,2048]{3,2,0,1:T(8,128)(2,1)}), bf16[32,2,16,2048]{3,2,0,1:T(8,128)(2,1)}) %all-reduce.2.cloned.1.call-update) | async-done | bytes 4194320 | tf_op jit(solution)/shard_map/psum | solution.py:41
  150.4 5.8 %fusion.30 = bf16[32,2,16,512]{3,2,0,1:T(8,128)(2,1)S(1)} fusion(bf16[2,2048,512]{2,1,0:T(8,128)(2,1)} %param.12, bf16[32,2,16,2048]{3,2,0,1:T(8,128)(2,1)} %all-reduce.2.cloned.1.call-done), kind=kOutput, calls=%fused_computation.30 | convolution fusion | flops 2154299392 | bytes 9437184 | tf_op jit(solution)/shard_map/sjch,jhd->sjcd/dot_general | solution.py:43
  156.2 0.0 copy-start.2
  156.2 0.0 copy-start.4
  156.2 0.1 copy.16
  156.3 24.6 %all_to_all.11 = bf16[32,2,16,512]{3,2,1,0:T(8,128)(2,1)S(1)} all-to-all(bf16[32,2,16,512]{3,2,1,0:T(8,128)(2,1)S(1)} %copy.16), channel_id=1, replica_groups=mesh['expert'=32,'tensor'=8] {'expert'}, dimensions={0} | all-to-all | bytes 2097152 | tf_op jit(solution)/shard_map/all_to_all | solution.py:20
  180.9 0.0 copy-done.2
  180.9 0.0 copy-done.4
  180.9 0.0 copy-start.3
  180.9 1.6 fusion.35
  182.5 0.0 all-gather.4.cloned.1.call-update
  182.5 0.0 all-gather.6.cloned.1.call-start
  182.6 0.7 all-gather.6.cloned.1.call-update
  183.3 0.0 all-gather.8.cloned.1.call-start
  183.3 0.5 all-gather.8.cloned.1.call-update
  183.8 0.2 reduce-scatter.2.cloned.1.call-start
  184.1 48.4 %all-gather.4.cloned.1.call-done = bf16[512,4096]{1,0:T(8,128)(2,1)} async-done(((bf16[512,512]{1,0:T(8,128)(2,1)}), bf16[512,4096]{1,0:T(8,128)(2,1)}) %all-gather.4.cloned.1.call-update) | async-done | bytes 4194320 | tf_op jit(solution)/shard_map/all_gather | solution.py:51
  232.4 3.1 fusion
  235.5 56.4 %all-gather.6.cloned.1.call-done = bf16[4096,1024]{1,0:T(8,128)(2,1)} async-done(((bf16[128,1024]{1,0:T(8,128)(2,1)}), bf16[4096,1024]{1,0:T(8,128)(2,1)}) %all-gather.6.cloned.1.call-update) | async-done | bytes 8388624 | tf_op jit(solution)/shard_map/all_gather | solution.py:25
  292.0 0.0 copy-done.3
  292.0 9.6 %fusion.21 = bf16[512,1024]{1,0:T(8,128)(2,1)S(1)} fusion(bf16[4096,1024]{1,0:T(8,128)(2,1)} %all-gather.6.cloned.1.call-done, bf16[512,4096]{1,0:T(8,128)(2,1)} %all-gather.4.cloned.1.call-done, f32[4096]{0:T(1024)S(1)} %copy-done.3, f32[512]{0:T(512)S(1)} %add_rsqrt_fusion), kind=kOutput, calls=%fused_computation.24 | convolution fusion | flops 4308074496 | bytes 13649920 | tf_op jit(solution)/shard_map/dot_general | solution.py:57
  301.6 50.4 %all-gather.8.cloned.1.call-done = bf16[4096,1024]{1,0:T(8,128)(2,1)} async-done(((bf16[128,1024]{1,0:T(8,128)(2,1)}), bf16[4096,1024]{1,0:T(8,128)(2,1)}) %all-gather.8.cloned.1.call-update) | async-done | bytes 8388624 | tf_op jit(solution)/shard_map/all_gather | solution.py:25
  352.0 9.5 %convolution_convert_fusion = bf16[512,4096]{1,0:T(8,128)(2,1)} fusion(bf16[512,1024]{1,0:T(8,128)(2,1)S(1)} %fusion.21, bf16[4096,1024]{1,0:T(8,128)(2,1)} %all-gather.8.cloned.1.call-done), kind=kOutput, calls=%fused_computation.6 | convolution fusion | flops 4297064448 | bytes 13631488 | tf_op jit(solution)/shard_map/dot_general | solution.py:65
  361.5 0.0 copy-start
  361.5 0.0 reduce-scatter.2.cloned.1.call-update
  361.5 54.7 %reduce-scatter.2.cloned.1.call-done = bf16[512,512]{1,0:T(8,128)(2,1)} async-done(((bf16[512,4096]{1,0:T(8,128)(2,1)}), bf16[512,512]{1,0:T(8,128)(2,1)}) %reduce-scatter.2.cloned.1.call-update) | async-done | bytes 524304 | tf_op jit(solution)/shard_map/reduce_scatter | solution.py:73
  416.3 0.0 copy-done
  416.3 2.0 add_convert_fusion
  (3 shorter events, 0.0 us)
Async XLA Ops:
  6.5 143.8 %all-reduce.2.cloned.1.call-start = ((), (), s32[]{:S(2)}) async-start(), calls=%async_computation.3 | async-start | bytes 8388608 | tf_op jit(solution)/shard_map/psum | solution.py:41
  8.7 29.2 %copy-start.1 = (bf16[2,512,2048]{2,1,0:T(8,128)(2,1)S(1)}, bf16[2,512,2048]{2,1,0:T(8,128)(2,1)}, u32[]{:S(2)}) copy-start(bf16[2,512,2048]{2,1,0:T(8,128)(2,1)} %param.11) | copy-start | bytes 12582916
  42.3 190.2 %all-gather.4.cloned.1.call-start = ((), (), s32[]{:S(2)}) async-start(), calls=%async_computation.4 | async-start | bytes 4718592 | tf_op jit(solution)/shard_map/all_gather | solution.py:51
  156.2 24.7 %copy-start.2 = (bf16[512,512]{1,0:T(8,128)(2,1)S(1)}, bf16[512,512]{1,0:T(8,128)(2,1)}, u32[]{:S(2)}) copy-start(bf16[512,512]{1,0:T(8,128)(2,1)} %param.8) | copy-start | bytes 1572868
  156.2 24.7 %copy-start.4 = (f32[512,1]{0,1:T(1,128)S(1)}, f32[512,1]{0,1:T(1,128)}, u32[]{:S(2)}) copy-start(f32[512,1]{0,1:T(1,128)} %param.10) | copy-start | bytes 6148
  180.9 111.0 %copy-start.3 = (f32[4096]{0:T(1024)S(1)}, f32[4096]{0:T(1024)}, u32[]{:S(2)}) copy-start(f32[4096]{0:T(1024)} %param.13) | copy-start | bytes 49156
  182.5 109.4 %all-gather.6.cloned.1.call-start = ((), (), s32[]{:S(2)}) async-start(), calls=%async_computation.5 | async-start | bytes 8650752 | tf_op jit(solution)/shard_map/all_gather | solution.py:25
  183.3 168.7 %all-gather.8.cloned.1.call-start = ((), (), s32[]{:S(2)}) async-start(), calls=%async_computation.6 | async-start | bytes 8650752 | tf_op jit(solution)/shard_map/all_gather | solution.py:25
  183.8 232.4 %reduce-scatter.2.cloned.1.call-start = ((), (), s32[]{:S(2)}) async-start(), calls=%async_computation.7 | async-start | bytes 4718592 | tf_op jit(solution)/shard_map/reduce_scatter | solution.py:73
  361.5 54.8 %copy-start = (bf16[512,512]{1,0:T(8,128)(2,1)S(1)}, bf16[512,512]{1,0:T(8,128)(2,1)}, u32[]{:S(2)}) copy-start(bf16[512,512]{1,0:T(8,128)(2,1)} %fusion.35) | copy-start | bytes 1572868
Sparse Core Ops, SparseCore 0:
  42.4 107.9 all-reduce.1
  182.6 49.7 all-gather.3
  235.0 56.9 all-gather.5
  294.4 57.5 all-gather.7
  361.6 54.5 reduce-scatter.1
where the time goes:
time: 425 us
  waiting for transfers between devices  319 us (75%)
  blocking collectives  50.2 us (12%)
  matrix products  32.6 us (8%)
  between operations  13.2 us (3%)
  other arithmetic  8.86 us (2%)
    psum x1, waiting for transfers between devices, shards(): lax.psum(partial_value.astype(jnp.bfloat16), 'tensor').astype(jnp.float32)  108 us
    all_gather x2, waiting for transfers between devices, gather_rows(): lax.all_gather(weight, 'expert', axis=0, tiled=True)  107 us
    reduce_scatter x1, waiting for transfers between devices, shards(): lax.psum_scatter(outputs.astype(jnp.bfloat16), 'tensor', scatter_dimensio...  54.7 us
    all_to_all x2, blocking collectives, trade(): lax.all_to_all(buffer, 'expert', split_axis=0, concat_axis=0, tiled=True)  50.2 us
    all_gather x1, waiting for transfers between devices, shards(): whole = lax.all_gather(mixed, 'tensor', axis=1, tiled=True)  48.4 us
    dot_general x1, matrix products, add_up(): return jnp.dot(normed, piece, preferred_element_type=jnp.float32)  9.58 us
    dot_general x1, matrix products, add_down(): lax.dot_general(ffn_active, piece, (((1,), (1,)), ((), ())), preferred_el...  9.54 us
  transfers between devices with their start and end apart: 5, of which 5 were waited for; matrix products, arithmetic and copies ran while one was open for 3% of the time, Pallas kernels for 0%

commit v1 on v0

--- a/solution.py
+++ b/solution.py
@@ -48,7 +48,20 @@
         selector, returned, (((0,), (0,)), ((), ())), preferred_element_type=jnp.float32
     )
     mixed = (tokens.astype(jnp.float32) + gates * routed).astype(jnp.bfloat16)
-    whole = lax.all_gather(mixed, "tensor", axis=1, tiled=True)
+    val2, small, then = (lax.psum(1, "tensor"), lax.axis_index("tensor"), mixed.shape[1])
+    steps_seen = [dev_j * val2 if p == 1 else dev_j for p, dev_j in enumerate(mixed.shape)]
+    odd = latest = mixed
+    whole = lax.dynamic_update_slice_in_dim(
+        jnp.zeros(steps_seen, mixed.dtype), mixed, small * then, axis=1
+    )
+    for pp in tuple(range(1, val2 // 2 + 1)):
+        odd = lax.ppermute(odd, "tensor", [(p, (p + 1) % val2) for p in range(val2)])
+        whole = lax.dynamic_update_slice_in_dim(whole, odd, (small - pp) % val2 * then, axis=1)
+        if 2 * pp < val2:
+            latest = lax.ppermute(latest, "tensor", [(p, (p - 1) % val2) for p in range(val2)])
+            whole = lax.dynamic_update_slice_in_dim(
+                whole, latest, (small + pp) % val2 * then, axis=1
+            )
     whole_f32 = whole.astype(jnp.float32)
     mean_square = jnp.mean(whole_f32 * whole_f32, axis=1, keepdims=True)
     normed = (whole_f32 * lax.rsqrt(mean_square + 1e-06) * norm_gain).astype(jnp.bfloat16)

time: 425 us -> 329 us (0.77)
  waiting for transfers between devices: 319 us -> 220 us
  blocking collectives: 50.2 us -> 25.6 us
  starting transfers between devices: 0.34 us -> 15.8 us
  local copies, waits for them, and re-layouts: 0.33 us -> 10.5 us
    all_gather x2, waiting for transfers between devices: 107 us -> 0.05 us  [gather_rows(): lax.all_gather(weight, 'expert', axis=0, tiled=True)]
    all_gather x1 -> x0, waiting for transfers between devices: 48.4 us -> none  [shards(): whole = lax.all_gather(mixed, 'tensor', axis=1, tiled=True)]
    ppermute x0 -> x7, waiting for transfers between devices: none -> 38.7 us  [the longest x4 38.7 us: shards(): lax.ppermute(odd, 'tensor', [(p, (p + 1) % val2) for p in range(val2)])]
    all_to_all x2 -> x1, blocking collectives: 50.2 us -> 25.6 us  [trade(): lax.all_to_all(buffer, 'expert', split_axis=0, concat_axis=0, tiled=True)]
    all_to_all x0 -> x1, waiting for transfers between devices: none -> 16.9 us  [trade(): lax.all_to_all(buffer, 'expert', split_axis=0, concat_axis=0, tiled=True)]
    ppermute x0 -> x7, starting transfers between devices: none -> 8.03 us  [the longest x3 8.02 us: shards(): lax.ppermute(latest, 'tensor', [(p, (p - 1) % val2) for p in range(val2)])]
    all_to_all x0 -> x1, starting transfers between devices: none -> 7.69 us  [trade(): lax.all_to_all(buffer, 'expert', split_axis=0, concat_axis=0, tiled=True)]
    dynamic_update_slice x0 -> x7, local copies, waits for them, and re-layouts: none -> 5.8 us  [the longest x4 3.32 us: shards(): lax.dynamic_update_slice_in_dim(whole, odd, (small - pp) % val2 * then, a...]
  transfers between devices with their start and end apart: 5 -> 12, of which waited for: 5 -> 7; matrix products, arithmetic and copies ran while one was open for 3% -> 9% of each run, Pallas kernels for 0% -> 0%
where the time goes in v1:
time: 329 us; the launch traced here: 328 us
  waiting for transfers between devices  220 us (67%)
  matrix products  33 us (10%)
  blocking collectives  25.6 us (8%)
  starting transfers between devices  15.8 us (5%)
  between operations  15 us (5%)
  local copies, waits for them, and re-layouts  10.5 us (3%)
  other arithmetic  8.12 us (2%)
    psum x1, waiting for transfers between devices, shards(): lax.psum(partial_value.astype(jnp.bfloat16), 'tensor').astype(jnp.float32)  107 us
    reduce_scatter x1, waiting for transfers between devices, shards(): lax.psum_scatter(outputs.astype(jnp.bfloat16), 'tensor', scatter_dimensio...  56.7 us
    ppermute x4, waiting for transfers between devices, shards(): lax.ppermute(odd, 'tensor', [(p, (p + 1) % val2) for p in range(val2)])  38.7 us
    all_to_all x1, blocking collectives, trade(): lax.all_to_all(buffer, 'expert', split_axis=0, concat_axis=0, tiled=True)  25.6 us
    all_to_all x1, waiting for transfers between devices, trade(): lax.all_to_all(buffer, 'expert', split_axis=0, concat_axis=0, tiled=True)  16.9 us
    dot_general x1, matrix products, add_up(): return jnp.dot(normed, piece, preferred_element_type=jnp.float32)  9.64 us
    dot_general x1, matrix products, add_down(): lax.dot_general(ffn_active, piece, (((1,), (1,)), ((), ())), preferred_el...  9.53 us
    ppermute x3, starting transfers between devices, shards(): lax.ppermute(latest, 'tensor', [(p, (p - 1) % val2) for p in range(val2)])  8.02 us
  transfers between devices with their start and end apart: 12, of which 7 were waited for; matrix products, arithmetic and copies ran while one was open for 9% of the time, Pallas kernels for 0%

profile of v1, /device:TPU:1, one launch (start us, length us, event | category | flops | bytes accessed | tf_op | source)
XLA Modules:
  0.0 328.4 jit_solution(6607001043702664230)
XLA Ops:
  7.4 0.7 fusion.48
  8.1 1.2 reduce-window.6
  9.3 0.2 slice_reduce_fusion
  9.5 0.9 fusion.47
  10.5 0.9 multiply_add_fusion
  11.4 1.8 fusion.24
  13.2 25.6 %all_to_all.10 = bf16[32,2,16,512]{3,2,1,0:T(8,128)(2,1)S(1)} all-to-all(bf16[32,2,16,512]{3,2,1,0:T(8,128)(2,1)S(1)} %bitcast.54), channel_id=1, replica_groups=mesh['expert'=32,'tensor'=8] {'expert'}, dimensions={0} | all-to-all | bytes 2097152 | tf_op jit(solution)/shard_map/all_to_all | solution.py:20
  38.8 4.3 %convert_bitcast_fusion = bf16[32,2,16,2048]{3,2,0,1:T(8,128)(2,1)} fusion(bf16[2,512,2048]{2,1,0:T(8,128)(2,1)S(1)} %copy-done.1, bf16[32,2,16,512]{3,2,1,0:T(8,128)(2,1)S(1)} %all_to_all.10), kind=kOutput, calls=%fused_computation.15 | convolution fusion | flops 2149580800 | bytes 9437184 | tf_op jit(solution)/shard_map/sjcd,jdh->sjch/dot_general | solution.py:38
  43.1 0.0 all-reduce.2.cloned.1.call-update
  43.1 0.0 all-gather.3.cloned.1.call-start
  43.2 0.5 all-gather.3.cloned.1.call-update
  43.7 0.0 all-gather.5.cloned.1.call-start
  43.7 0.5 all-gather.5.cloned.1.call-update
  44.3 106.9 %all-reduce.2.cloned.1.call-done = bf16[32,2,16,2048]{3,2,0,1:T(8,128)(2,1)} async-done(((bf16[32,2,16,2048]{3,2,0,1:T(8,128)(2,1)}), bf16[32,2,16,2048]{3,2,0,1:T(8,128)(2,1)}) %all-reduce.2.cloned.1.call-update) | async-done | bytes 4194320 | tf_op jit(solution)/shard_map/psum | solution.py:41
  151.2 6.1 %fusion.30 = bf16[32,2,16,512]{3,2,0,1:T(8,128)(2,1)S(1)} fusion(bf16[2,2048,512]{2,1,0:T(8,128)(2,1)} %param.12, bf16[32,2,16,2048]{3,2,0,1:T(8,128)(2,1)} %all-reduce.2.cloned.1.call-done), kind=kOutput, calls=%fused_computation.30 | convolution fusion | flops 2154299392 | bytes 9437184 | tf_op jit(solution)/shard_map/sjch,jhd->sjcd/dot_general | solution.py:43
  157.3 0.0 copy-start
  157.4 1.0 copy.26
  158.4 7.7 %all-to-all-start.1 = ((bf16[32,2,16,512]{3,2,1,0:T(8,128)(2,1)}), bf16[32,2,16,512]{3,2,1,0:T(8,128)(2,1)S(1)}, u32[]{:S(2)}, u32[]{:S(2)}) async-start(bf16[32,2,16,512]{3,2,1,0:T(8,128)(2,1)} %copy.26), calls=%async_computation.1 | async-start | bytes 2097152 | tf_op jit(solution)/shard_map/all_to_all | solution.py:20
  166.1 0.0 reduce-scatter.2.cloned.1.call-start
  166.2 0.2 copy.23
  166.4 16.9 %all-to-all-done.1 = bf16[32,2,16,512]{3,2,1,0:T(8,128)(2,1)S(1)} async-done(((bf16[32,2,16,512]{3,2,1,0:T(8,128)(2,1)}), bf16[32,2,16,512]{3,2,1,0:T(8,128)(2,1)S(1)}, u32[]{:S(2)}, u32[]{:S(2)}) %all-to-all-start.1) | async-done | bytes 1048608 | tf_op jit(solution)/shard_map/all_to_all | solution.py:20
  183.3 2.2 broadcast_in_dim.2
  185.5 1.6 constant_dynamic-update-slice_fusion.7
  187.1 2.7 collective-permute-start.1
  189.8 11.6 %collective-permute-done = bf16[512,512]{0,1:T(8,128)(2,1)S(1)} collective-permute-done((bf16[512,512]{0,1:T(8,128)(2,1)S(1)}, bf16[512,512]{0,1:T(8,128)(2,1)S(1)}, u32[]{:S(2)}, u32[]{:S(2)}) %collective-permute-start) | collective-permute-done | bytes 524320 | tf_op jit(solution)/shard_map/ppermute | solution.py:58
  201.4 0.0 collective-permute-start.2
  201.4 0.0 collective-permute-done.1
  201.4 2.7 collective-permute-start.3
  204.1 10.7 %collective-permute-done.2 = bf16[512,512]{0,1:T(8,128)(2,1)S(1)} collective-permute-done((bf16[512,512]{0,1:T(8,128)(2,1)S(1)}, bf16[512,512]{0,1:T(8,128)(2,1)S(1)}, u32[]{:S(2)}, u32[]{:S(2)}) %collective-permute-start.2) | collective-permute-done | bytes 524320 | tf_op jit(solution)/shard_map/ppermute | solution.py:58
  214.8 2.7 collective-permute-start.5
  217.5 0.8 constant_dynamic-update-slice_fusion.6
  218.3 9.0 %collective-permute-done.4 = bf16[512,512]{0,1:T(8,128)(2,1)S(1)} collective-permute-done((bf16[512,512]{0,1:T(8,128)(2,1)S(1)}, bf16[512,512]{0,1:T(8,128)(2,1)S(1)}, u32[]{:S(2)}, u32[]{:S(2)}) %collective-permute-start.4) | collective-permute-done | bytes 524320 | tf_op jit(solution)/shard_map/ppermute | solution.py:58
  227.3 0.8 constant_dynamic-update-slice_fusion.5
  228.1 0.8 constant_dynamic-update-slice_fusion.4
  228.9 0.8 constant_dynamic-update-slice_fusion.3
  229.8 0.8 constant_dynamic-update-slice_fusion.2
  230.6 0.8 constant_dynamic-update-slice_fusion.1
  231.4 7.4 %collective-permute-done.6 = bf16[512,512]{0,1:T(8,128)(2,1)S(1)} collective-permute-done((bf16[512,512]{0,1:T(8,128)(2,1)S(1)}, bf16[512,512]{0,1:T(8,128)(2,1)S(1)}, u32[]{:S(2)}, u32[]{:S(2)}) %collective-permute-start.6) | collective-permute-done | bytes 524320 | tf_op jit(solution)/shard_map/ppermute | solution.py:58
  238.8 0.8 constant_dynamic-update-slice_fusion
  239.7 3.1 fusion
  242.8 0.0 all-gather.3.cloned.1.call-done
  242.8 9.6 %fusion.21.clone.4 = bf16[512,1024]{1,0:T(8,128)(2,1)S(1)} fusion(bf16[4096,1024]{1,0:T(8,128)(2,1)} %all-gather.3.cloned.1.call-done, bf16[512,4096]{0,1:T(8,128)(2,1)} %constant_dynamic-update-slice_fusion, f32[4096]{0:T(1024)S(1)} %copy-done.2, f32[512]{0:T(512)S(1)} %add_rsqrt_fusion), kind=kOutput, calls=%fused_computation.24.clone.clone.clone.1 | convolution fusion | flops 4308074496 | bytes 13649920 | tf_op jit(solution)/shard_map/dot_general | solution.py:70
  252.5 0.0 all-gather.5.cloned.1.call-done
  252.5 9.5 %convolution_convert_fusion = bf16[512,4096]{0,1:T(8,128)(2,1)} fusion(bf16[4096,1024]{1,0:T(8,128)(2,1)} %all-gather.5.cloned.1.call-done, bf16[512,1024]{1,0:T(8,128)(2,1)S(1)} %fusion.21.clone.4), kind=kOutput, calls=%fused_computation.6 | convolution fusion | flops 4297064448 | bytes 13631488 | tf_op jit(solution)/shard_map/dot_general | solution.py:78
  262.0 0.0 reduce-scatter.2.cloned.1.call-update
  262.1 56.7 %reduce-scatter.2.cloned.1.call-done = bf16[512,512]{0,1:T(8,128)(2,1)} async-done(((bf16[512,4096]{0,1:T(8,128)(2,1)}), bf16[512,512]{0,1:T(8,128)(2,1)}) %reduce-scatter.2.cloned.1.call-update) | async-done | bytes 524304 | tf_op jit(solution)/shard_map/reduce_scatter | solution.py:86
  318.8 1.2 add_convert_fusion
  319.9 1.0 copy.28
  (16 shorter events, 0.1 us)
Async XLA Ops:
  7.4 143.8 %all-reduce.2.cloned.1.call-start = ((), (), s32[]{:S(2)}) async-start(), calls=%async_computation.3 | async-start | bytes 8388608 | tf_op jit(solution)/shard_map/psum | solution.py:41
  9.5 29.2 %copy-start.1 = (bf16[2,512,2048]{2,1,0:T(8,128)(2,1)S(1)}, bf16[2,512,2048]{2,1,0:T(8,128)(2,1)}, u32[]{:S(2)}) copy-start(bf16[2,512,2048]{2,1,0:T(8,128)(2,1)} %param.11) | copy-start | bytes 12582916
  43.1 199.7 %all-gather.3.cloned.1.call-start = ((), (), s32[]{:S(2)}) async-start(), calls=%async_computation.4 | async-start | bytes 8650752 | tf_op jit(solution)/shard_map/all_gather | solution.py:25
  43.7 208.8 %all-gather.5.cloned.1.call-start = ((), (), s32[]{:S(2)}) async-start(), calls=%async_computation.5 | async-start | bytes 8650752 | tf_op jit(solution)/shard_map/all_gather | solution.py:25
  157.3 8.8 %copy-start = (bf16[512,512]{1,0:T(8,128)(2,1)S(1)}, bf16[512,512]{1,0:T(8,128)(2,1)}, u32[]{:S(2)}) copy-start(bf16[512,512]{1,0:T(8,128)(2,1)} %param.8) | copy-start | bytes 1572868
  158.4 27.1 %copy-start.3 = (f32[512,1]{0,1:T(1,128)S(1)}, f32[512,1]{0,1:T(1,128)}, u32[]{:S(2)}) copy-start(f32[512,1]{0,1:T(1,128)} %param.10) | copy-start | bytes 6148
  158.4 24.9 %all-to-all-start.1 = ((bf16[32,2,16,512]{3,2,1,0:T(8,128)(2,1)}), bf16[32,2,16,512]{3,2,1,0:T(8,128)(2,1)S(1)}, u32[]{:S(2)}, u32[]{:S(2)}) async-start(bf16[32,2,16,512]{3,2,1,0:T(8,128)(2,1)} %copy.26), calls=%async_computation.1 | async-start | bytes 2097152 | tf_op jit(solution)/shard_map/all_to_all | solution.py:20
  166.1 152.7 %reduce-scatter.2.cloned.1.call-start = ((), (), s32[]{:S(2)}) async-start(), calls=%async_computation.6 | async-start | bytes 4718592 | tf_op jit(solution)/shard_map/reduce_scatter | solution.py:86
  187.1 14.3 %collective-permute-start = (bf16[512,512]{0,1:T(8,128)(2,1)S(1)}, bf16[512,512]{0,1:T(8,128)(2,1)S(1)}, u32[]{:S(2)}, u32[]{:S(2)}) collective-permute-start(bf16[512,512]{0,1:T(8,128)(2,1)S(1)} %get-tuple-element.6), channel_id=1, source_target_pairs={{0,1},{1,2},{2,3},{3,4},{4,5},{5,6},{6,7},{7,0},{8,9},{9,10},{10,1... | collective-permute-start | bytes 1572872 | tf_op jit(solution)/shard_map/ppermute | solution.py:58
  187.1 14.3 %collective-permute-start.1 = (bf16[512,512]{0,1:T(8,128)(2,1)S(1)}, bf16[512,512]{0,1:T(8,128)(2,1)S(1)}, u32[]{:S(2)}, u32[]{:S(2)}) collective-permute-start(bf16[512,512]{0,1:T(8,128)(2,1)S(1)} %get-tuple-element.6), channel_id=1, source_target_pairs={{0,7},{1,0},{2,1},{3,2},{4,3},{5,4},{6,5},{7,6},{8,15},{9,8},{10,9... | collective-permute-start | bytes 1572872 | tf_op jit(solution)/shard_map/ppermute | solution.py:61
  201.4 13.4 %collective-permute-start.2 = (bf16[512,512]{0,1:T(8,128)(2,1)S(1)}, bf16[512,512]{0,1:T(8,128)(2,1)S(1)}, u32[]{:S(2)}, u32[]{:S(2)}) collective-permute-start(bf16[512,512]{0,1:T(8,128)(2,1)S(1)} %collective-permute-done), channel_id=1, source_target_pairs={{0,1},{1,2},{2,3},{3,4},{4,5},{5,6},{6,7},{7,0},{8,9},{9,10},{10,1... | collective-permute-start | bytes 1572872 | tf_op jit(solution)/shard_map/ppermute | solution.py:58
  201.4 13.4 %collective-permute-start.3 = (bf16[512,512]{0,1:T(8,128)(2,1)S(1)}, bf16[512,512]{0,1:T(8,128)(2,1)S(1)}, u32[]{:S(2)}, u32[]{:S(2)}) collective-permute-start(bf16[512,512]{0,1:T(8,128)(2,1)S(1)} %collective-permute-done.1), channel_id=1, source_target_pairs={{0,7},{1,0},{2,1},{3,2},{4,3},{5,4},{6,5},{7,6},{8,15},{9,8},{10,9... | collective-permute-start | bytes 1572872 | tf_op jit(solution)/shard_map/ppermute | solution.py:61
  214.8 12.5 %collective-permute-start.4 = (bf16[512,512]{0,1:T(8,128)(2,1)S(1)}, bf16[512,512]{0,1:T(8,128)(2,1)S(1)}, u32[]{:S(2)}, u32[]{:S(2)}) collective-permute-start(bf16[512,512]{0,1:T(8,128)(2,1)S(1)} %collective-permute-done.2), channel_id=1, source_target_pairs={{0,1},{1,2},{2,3},{3,4},{4,5},{5,6},{6,7},{7,0},{8,9},{9,10},{10,1... | collective-permute-start | bytes 1572872 | tf_op jit(solution)/shard_map/ppermute | solution.py:58
  214.8 15.8 %collective-permute-start.5 = (bf16[512,512]{0,1:T(8,128)(2,1)S(1)}, bf16[512,512]{0,1:T(8,128)(2,1)S(1)}, u32[]{:S(2)}, u32[]{:S(2)}) collective-permute-start(bf16[512,512]{0,1:T(8,128)(2,1)S(1)} %collective-permute-done.3), channel_id=1, source_target_pairs={{0,7},{1,0},{2,1},{3,2},{4,3},{5,4},{6,5},{7,6},{8,15},{9,8},{10,9... | collective-permute-start | bytes 1572872 | tf_op jit(solution)/shard_map/ppermute | solution.py:61
  227.3 11.6 %collective-permute-start.6 = (bf16[512,512]{0,1:T(8,128)(2,1)S(1)}, bf16[512,512]{0,1:T(8,128)(2,1)S(1)}, u32[]{:S(2)}, u32[]{:S(2)}) collective-permute-start(bf16[512,512]{0,1:T(8,128)(2,1)S(1)} %collective-permute-done.4), channel_id=1, source_target_pairs={{0,1},{1,2},{2,3},{3,4},{4,5},{5,6},{6,7},{7,0},{8,9},{9,10},{10,1... | collective-permute-start | bytes 1572872 | tf_op jit(solution)/shard_map/ppermute | solution.py:58
  228.9 13.9 %copy-start.2 = (f32[4096]{0:T(1024)S(1)}, f32[4096]{0:T(1024)}, u32[]{:S(2)}) copy-start(f32[4096]{0:T(1024)} %param.13) | copy-start | bytes 49156
Sparse Core Ops, SparseCore 0:
  43.2 107.9 all-reduce.1
  262.2 56.5 reduce-scatter.1
Sparse Core Ops, SparseCore 1:
  46.1 57.1 all-gather.2
  105.7 57.4 all-gather.4
